TPU v7x, 32 devices: a whole 2x2x4 slice. The times are simulated.
32 devices in a mesh: tm: 4 (over x, core), space: 8 (over z, y).
Axes of the slice: x: 2, y: 2, z: 4, core: 2. Of those that a mesh axis runs over, the one named last changes fastest.
Arguments:
- starts: float32 [4, 32, 256, 384], P('tm', 'space'), may hold values from -18 to 18, as said below
- material: int32 [32, 256, 384], P('space'), may hold values from 0 to 7
- conductivity: float32 [8], replicated, may hold values from 0.3 to 3, as said below
Outputs:
- new_starts: float32 [4, 32, 256, 384], P('tm', 'space')
- coarse_path: float32 [4, 8, 64, 96], P('tm')
Inputs may be any that keep to these rules, and one draw needn't show every extreme that they name: `starts`: start states of order one. `conductivity`: positive conductivities.
All inputs are finite; a program needn't handle non-finite values.
Results may differ from a plain program's by a relative error of at most 0.0001.
Values sent between devices are 32-bit elements; how exact they have to be, the bound alone decides.
A program may use at most 128 MiB of HBM per device.

v0:
```python
import jax
import jax.numpy as jnp
from jax import lax
from jax.sharding import PartitionSpec as P

FACTOR = 4
SUBSTEPS = 2
SWEEPS = 2
JACOBI = 3
fine_step = 0.15
coarse_rate = 0.3
face_offsets = ((0, 1, 1), (2, 1, 1), (1, 0, 1), (1, 2, 1), (1, 1, 0), (1, 1, 2))


def extended(x, sides, width):
    for axis, dim in sides:
        peers, length = (lax.axis_size(axis), x.shape[dim])
        up = [(i, (i + 1) % peers) for i in range(peers - 1)]
        down = [(j, i) for i, j in up]
        last = lax.slice_in_dim(x, length - width, length, axis=dim)
        leading = lax.slice_in_dim(x, 0, width, axis=dim)
        before = lax.ppermute(last, axis, up)
        after = lax.ppermute(leading, axis, down)
        x = jnp.concatenate([before, x, after], axis=dim)
    return x


def shifted(x, axis, by):
    peers = lax.axis_size(axis)
    pairs = [(i, i + by) for i in range(peers) if 0 <= i + by < peers]
    return lax.ppermute(x, axis, pairs)


def window(padded, offsets, cells):
    return padded[
        offsets[0] : offsets[0] + cells[0],
        offsets[1] : offsets[1] + cells[1],
        offsets[2] : offsets[2] + cells[2],
    ]


def laplace_apply(padded, cells):
    summed = jnp.zeros(cells, jnp.float32)
    for shift_x in range(3):
        for shift_y in range(3):
            for shift_z in range(3):
                moved_axes = int(shift_x != 1) + int(shift_y != 1) + int(shift_z != 1)
                if moved_axes == 0:
                    continue
                weight = 0.5 ** (moved_axes - 1)
                summed = summed + weight * window(padded, (shift_x, shift_y, shift_z), cells)
    return 14.0 * window(padded, (1, 1, 1), cells) - summed


def operate(vector, root_cond):
    scaled = root_cond * vector
    padded = extended(scaled, (("space", 0),), 1)
    padded = jnp.pad(padded, ((0, 0), (1, 1), (1, 1)))
    return vector + fine_step * root_cond * laplace_apply(padded, vector.shape)


def grid_squares(resid):
    return lax.psum(jnp.sum(resid * resid), "space")


def grid_curvature(direction, image):
    return lax.psum(jnp.sum(direction * image), "space")


def substep(rhs_field, root_cond):
    iterate = rhs_field
    resid = rhs_field - operate(iterate, root_cond)
    direction = resid
    norm_now = grid_squares(resid)
    for sweep_index in range(SWEEPS):
        image = operate(direction, root_cond)
        step_len = norm_now / grid_curvature(direction, image)
        iterate = iterate + step_len * direction
        resid = resid - step_len * image
        if sweep_index + 1 < SWEEPS:
            norm_next = grid_squares(resid)
            direction = resid + norm_next / norm_now * direction
            norm_now = norm_next
    return iterate


def propagate(start_field, root_cond):
    current = start_field
    for step_index in range(SUBSTEPS):
        current = substep(current, root_cond)
    return current


def restrict(fine_field):
    size_x, size_y, size_z = fine_field.shape
    blocks = fine_field.reshape(
        size_x // FACTOR, FACTOR, size_y // FACTOR, FACTOR, size_z // FACTOR, FACTOR
    )
    return jnp.mean(blocks, axis=(1, 3, 5))


def prolong(coarse_field):
    size_x, size_y, size_z = coarse_field.shape
    spread = jnp.broadcast_to(
        coarse_field[:, None, :, None, :, None], (size_x, FACTOR, size_y, FACTOR, size_z, FACTOR)
    )
    return spread.reshape(size_x * FACTOR, size_y * FACTOR, size_z * FACTOR)


def coarse_setup(coarse_k):
    padded_k = jnp.pad(coarse_k, 1, mode="edge")
    face_coefs = []
    diagonal = jnp.ones(coarse_k.shape, jnp.float32)
    for offsets in face_offsets:
        coef = coarse_rate * 0.5 * (coarse_k + window(padded_k, offsets, coarse_k.shape))
        face_coefs.append(coef)
        diagonal = diagonal + coef
    return (face_coefs, diagonal)


def coarse_step(source, face_coefs, diagonal):
    iterate = source
    for sweep_index in range(JACOBI):
        padded = jnp.pad(iterate, 1)
        summed = jnp.zeros(source.shape, jnp.float32)
        for coef, offsets in zip(face_coefs, face_offsets):
            summed = summed + coef * window(padded, offsets, source.shape)
        iterate = (source + summed) / diagonal
    return iterate


def local(starts, material, conductivity):
    start_field = starts[0]
    conduct = jnp.zeros(start_field.shape, jnp.float32)
    for region in range(conductivity.shape[0]):
        conduct = conduct + jnp.where(material == region, conductivity[region], 0.0)
    root_cond = jnp.sqrt(conduct)
    coarse_start, coarse_k = (
        lax.all_gather(restrict(start_field), "space", axis=0, tiled=True),
        lax.all_gather(restrict(conduct), "space", axis=0, tiled=True),
    )
    face_coefs, diagonal = coarse_setup(coarse_k)
    coarse_old = coarse_step(coarse_start, face_coefs, diagonal)
    fine_end = propagate(start_field, root_cond)
    tm_index = lax.axis_index("tm")
    slice_count = lax.axis_size("tm")
    local_end = restrict(fine_end)
    coarse_end = lax.all_gather(local_end, "space", axis=0, tiled=True)
    jump_term = coarse_end - coarse_old
    coarse_rows = local_end.shape[0]
    carry_start = jnp.where(tm_index == 0, coarse_start, jnp.zeros_like(coarse_start))

    def relay_turn(turn_index, carry_in):
        stepped = coarse_step(carry_in, face_coefs, diagonal) + jump_term
        arrived = shifted(stepped, "tm", 1)
        return jnp.where(tm_index == turn_index + 1, arrived, carry_in)

    carry_own = lax.fori_loop(0, slice_count - 1, relay_turn, carry_start)
    path_own = coarse_step(carry_own, face_coefs, diagonal) + jump_term
    slab_offset = lax.axis_index("space") * coarse_rows
    path_slab = lax.dynamic_slice_in_dim(path_own, slab_offset, coarse_rows, 0)
    corrected = fine_end + prolong(path_slab - local_end)
    received = shifted(corrected, "tm", 1)
    new_field = jnp.where(tm_index == 0, start_field, received)
    return (new_field[None], path_own[None])


def solution(mesh):
    return jax.shard_map(
        local,
        mesh=mesh,
        in_specs=(P("tm", "space", None, None), P("space", None, None), P()),
        out_specs=(P("tm", "space", None, None), P("tm", None, None, None)),
        check_vma=False,
    )
```

profile of v0, /device:TPU:1, one launch (start us, length us, event | category | flops | bytes accessed | tf_op | source)
XLA Modules:
  0.0 589.1 jit_solution(5427695950292236274)
XLA Ops:
  2.3 8.4 %bitcast_multiply_fusion = f32[4,256,384]{2,1,0:T(8,128)S(1)} fusion(f32[1,4,256,384]{3,2,1,0:T(8,128)} %param.5, f32[]{:T(128)} %bitcast.8, s32[4,256,384]{2,1,0:T(8,128)} %param.6, f32[]{:T(128)} %bitcast.7, f32[]{:T(128)} %bitcast.6, f32[]{:T(128)} %bitcast.5, f32[]{:T(128)} %bitcast.4, f32[]{:T(128)} %bitcast.3, f32[]{:T(128)} %bitcast.2, f32[]{:T(128)} %bitcast.1), kind=kLoop, calls=%fused_computation.382 | loop fusion | flops 9437184 | bytes 4718624 | tf_op jit(solution)/shard_map/mul | solution.py:56
  12.0 4.6 collective-permute-start.1
  16.7 6.9 %collective-permute-done.2 = f32[1,256,384]{2,1,0:T(8,128)S(1)} collective-permute-done((f32[1,256,384]{2,1,0:T(8,128)S(1)}, f32[1,256,384]{2,1,0:T(8,128)S(1)}, u32[]{:S(2)}, u32[]{:S(2)}) %collective-permute-start.2) | collective-permute-done | bytes 393248 | tf_op jit(solution)/shard_map/ppermute | solution.py:23
  23.5 9.3 %collective-permute-done.1 = f32[1,256,384]{2,1,0:T(8,128)S(1)} collective-permute-done((f32[1,256,384]{2,1,0:T(8,128)S(1)}, f32[1,256,384]{2,1,0:T(8,128)S(1)}, u32[]{:S(2)}, u32[]{:S(2)}) %collective-permute-start.1) | collective-permute-done | bytes 393248 | tf_op jit(solution)/shard_map/ppermute | solution.py:22
  34.6 14.8 %sqrt_multiply_fusion.4 = (f32[4,256,384]{2,1,0:T(8,128)}, f32[4,256,384]{2,1,0:T(8,128)}) fusion(f32[]{:T(128)} %bitcast.8, s32[4,256,384]{2,1,0:T(8,128)} %param.6, f32[]{:T(128)} %bitcast.7, f32[]{:T(128)} %bitcast.6, f32[]{:T(128)} %bitcast.5, f32[]{:T(128)} %bitcast.4, f32[]{:T(128)} %bitcast.3, f32[]{:T(128)} %bitcast.2, f32[]{:T(128)} %bitcast.1, ...), kind=kLoop, calls=%fused_computation.402 | loop fusion | flops 30277632 | bytes 46399520 | tf_op jit(solution)/shard_map/mul | solution.py:56
  52.1 4.8 collective-permute-start.3
  56.8 7.1 %collective-permute-done.4 = f32[1,256,384]{2,1,0:T(8,128)S(1)} collective-permute-done((f32[1,256,384]{2,1,0:T(8,128)S(1)}, f32[1,256,384]{2,1,0:T(8,128)S(1)}, u32[]{:S(2)}, u32[]{:S(2)}) %collective-permute-start.4) | collective-permute-done | bytes 393248 | tf_op jit(solution)/shard_map/ppermute | solution.py:23
  63.9 9.1 %collective-permute-done.3 = f32[1,256,384]{2,1,0:T(8,128)S(1)} collective-permute-done((f32[1,256,384]{2,1,0:T(8,128)S(1)}, f32[1,256,384]{2,1,0:T(8,128)S(1)}, u32[]{:S(2)}, u32[]{:S(2)}) %collective-permute-start.3) | collective-permute-done | bytes 393248 | tf_op jit(solution)/shard_map/ppermute | solution.py:22
  74.1 15.3 %multiply_reduce_fusion.4 = (f32[]{:T(128)}, f32[]{:T(128)}, f32[4,256,384]{2,1,0:T(8,128)}) fusion(f32[4,256,384]{2,1,0:T(8,128)} %get-tuple-element.313, f32[6,258,386]{2,1,0:T(8,128)S(1)} %select_maximum_fusion.8, f32[1,256,384]{2,1,0:T(8,128)} %copy-done.29, f32[4,256,384]{2,1,0:T(8,128)} %get-tuple-element.312, f32[1,256,384]{2,1,0:T(8,128)} %copy-done.32, ...), kind=kLoop, calls=%fused_computation.394 | loop fusion | flops 31064064 | bytes 44826664 | tf_op jit(solution)/shard_map/reduce_sum | solution.py:67
  89.3 17.0 %all-reduce.16 = (f32[]{:T(128)}, f32[]{:T(128)}) all-reduce(f32[]{:T(128)} %get-tuple-element.270, f32[]{:T(128)} %get-tuple-element.269), channel_id=1, replica_groups=mesh['tm'=4,'space'=8] {'space'}, use_global_device_ids=true, to_apply=%region_1.2 | all-reduce | flops 2 | bytes 16 | tf_op jit(solution)/shard_map/psum | solution.py:63
  110.6 14.4 %psum.58 = f32[]{:T(128)} all-reduce(f32[]{:T(128)} %multiply_reduce_fusion.3), channel_id=1, replica_groups=mesh['tm'=4,'space'=8] {'space'}, use_global_device_ids=true, to_apply=%region_5.6 | all-reduce | flops 1 | bytes 8 | tf_op jit(solution)/shard_map/psum | solution.py:63
  126.4 8.1 %sqrt_multiply_fusion.3 = f32[4,256,384]{2,1,0:T(8,128)S(1)} fusion(f32[4,256,384]{2,1,0:T(8,128)S(1)} %copy-done.13, f32[]{:T(128)S(6)} %div.82, f32[4,256,384]{2,1,0:T(8,128)} %get-tuple-element.311, f32[]{:T(128)S(6)} %div.81, f32[]{:T(128)} %bitcast.8, s32[4,256,384]{2,1,0:T(8,128)S(1)} %copy-done, f32[]{:T(128)} %bitcast.7, f32[]{:T(128)} %bitcast.6, ...), kind=kLoop, calls=%fused_computation.401 | loop fusion | flops 11010048 | bytes 6291496 | tf_op jit(solution)/shard_map/mul | solution.py:56
  135.9 4.2 collective-permute-start.5
  143.3 9.0 %collective-permute-done.5 = f32[1,256,384]{2,1,0:T(8,128)S(1)} collective-permute-done((f32[1,256,384]{2,1,0:T(8,128)S(1)}, f32[1,256,384]{2,1,0:T(8,128)S(1)}, u32[]{:S(2)}, u32[]{:S(2)}) %collective-permute-start.5) | collective-permute-done | bytes 393248 | tf_op jit(solution)/shard_map/ppermute | solution.py:22
  154.0 14.7 %fusion.43 = f32[]{:T(128)} fusion(f32[6,258,386]{2,1,0:T(8,128)S(1)} %select_maximum_fusion.6, f32[1,256,384]{2,1,0:T(8,128)} %copy-done.33, f32[4,256,384]{2,1,0:T(8,128)} %copy-done.23, f32[1,256,384]{2,1,0:T(8,128)} %copy-done.36, f32[4,256,384]{2,1,0:T(8,128)} %get-tuple-element.313, f32[]{:T(128)S(6)} %div.82, f32[4,256,384]{2,1,0:T(8,128)} %get-tuple-element.311, ...), kind=kLoop, calls=%fused_computation.82 | loop fusion | flops 31850496 | bytes 44826668 | tf_op jit(solution)/shard_map/reduce_sum | solution.py:67
  168.8 16.6 %psum.59 = f32[]{:T(128)} all-reduce(f32[]{:T(128)} %fusion.43), channel_id=1, replica_groups=mesh['tm'=4,'space'=8] {'space'}, use_global_device_ids=true, to_apply=%region_7.8 | all-reduce | flops 1 | bytes 8 | tf_op jit(solution)/shard_map/psum | solution.py:67
  186.7 10.9 %sqrt_multiply_fusion.2 = (f32[4,256,384]{2,1,0:T(8,128)S(1)}, f32[4,256,384]{2,1,0:T(8,128)}) fusion(f32[]{:T(128)} %bitcast.8, s32[4,256,384]{2,1,0:T(8,128)} %param.6, f32[]{:T(128)} %bitcast.7, f32[]{:T(128)} %bitcast.6, f32[]{:T(128)} %bitcast.5, f32[]{:T(128)} %bitcast.4, f32[]{:T(128)} %bitcast.3, f32[]{:T(128)} %bitcast.2, f32[]{:T(128)} %bitcast.1, ...), kind=kLoop, calls=%fused_computation.400 | loop fusion | flops 12582912 | bytes 9437228 | tf_op jit(solution)/shard_map/mul | solution.py:56
  198.9 4.2 collective-permute-start.7
  209.5 14.9 %sqrt_multiply_fusion.1 = (f32[4,256,384]{2,1,0:T(8,128)}, f32[4,256,384]{2,1,0:T(8,128)}) fusion(f32[]{:T(128)} %bitcast.8, s32[4,256,384]{2,1,0:T(8,128)} %param.6, f32[]{:T(128)} %bitcast.7, f32[]{:T(128)} %bitcast.6, f32[]{:T(128)} %bitcast.5, f32[]{:T(128)} %bitcast.4, f32[]{:T(128)} %bitcast.3, f32[]{:T(128)} %bitcast.2, f32[]{:T(128)} %bitcast.1, ...), kind=kLoop, calls=%fused_computation.399 | loop fusion | flops 30277632 | bytes 46399520 | tf_op jit(solution)/shard_map/mul | solution.py:56
  227.0 5.2 collective-permute-start.9
  232.3 14.7 %reduce_sum.129 = f32[64,4,96,4]{3,2,1,0:T(8,128)} reshape(f32[256,384]{1,0:T(8,128)S(1)} %reduce_sum.128) | data formatting | bytes 786432 | tf_op jit(solution)/shard_map/reduce_sum | solution.py:99
  246.9 5.7 reduce_sum.130
  252.7 24.9 %all-gather = f32[512,96]{1,0:T(8,128)S(1)} all-gather(f32[64,96]{1,0:T(8,128)S(1)} %broadcast_multiply_fusion.2), channel_id=2, replica_groups=mesh['tm'=4,'space'=8] {'space'}, dimensions={0}, use_global_device_ids=true | all-gather | bytes 221184 | tf_op jit(solution)/shard_map/all_gather | solution.py:139
  281.0 15.3 %multiply_reduce_fusion.1 = (f32[]{:T(128)}, f32[]{:T(128)}, f32[4,256,384]{2,1,0:T(8,128)}) fusion(f32[4,256,384]{2,1,0:T(8,128)} %get-tuple-element.308, f32[6,258,386]{2,1,0:T(8,128)S(1)} %select_maximum_fusion.2, f32[1,256,384]{2,1,0:T(8,128)} %copy-done.28, f32[4,256,384]{2,1,0:T(8,128)} %get-tuple-element.307, ...), kind=kLoop, calls=%fused_computation.389 | loop fusion | flops 31064064 | bytes 44826664 | tf_op jit(solution)/shard_map/reduce_sum | solution.py:67
  296.3 17.0 %all-reduce.15 = (f32[]{:T(128)}, f32[]{:T(128)}) all-reduce(f32[]{:T(128)} %get-tuple-element.268, f32[]{:T(128)} %get-tuple-element.267), channel_id=1, replica_groups=mesh['tm'=4,'space'=8] {'space'}, use_global_device_ids=true, to_apply=%region_9.10 | all-reduce | flops 2 | bytes 16 | tf_op jit(solution)/shard_map/psum | solution.py:63
  317.7 14.7 %psum.62 = f32[]{:T(128)} all-reduce(f32[]{:T(128)} %multiply_reduce_fusion), channel_id=1, replica_groups=mesh['tm'=4,'space'=8] {'space'}, use_global_device_ids=true, to_apply=%region_13.14 | all-reduce | flops 1 | bytes 8 | tf_op jit(solution)/shard_map/psum | solution.py:63
  333.7 9.0 %fusion.280 = (f32[256,384]{1,0:T(8,128)}, f32[4,256,384]{2,1,0:T(8,128)S(1)}) fusion(f32[]{:T(128)} %bitcast.8, s32[4,256,384]{2,1,0:T(8,128)S(1)} %copy-done.1, f32[]{:T(128)} %bitcast.7, f32[]{:T(128)} %bitcast.6, f32[]{:T(128)} %bitcast.5, f32[]{:T(128)} %bitcast.4, f32[]{:T(128)} %bitcast.3, f32[]{:T(128)} %bitcast.2, f32[]{:T(128)} %bitcast.1, ...), kind=kLoop, calls=%fused_computation.563 | loop fusion | flops 11304960 | bytes 6684712 | tf_op jit(solution)/shard_map/reduce_sum | solution.py:99
  345.1 4.7 collective-permute-start.11
  349.9 14.6 %reduce_sum.132 = f32[64,4,96,4]{3,2,1,0:T(8,128)} reshape(f32[256,384]{1,0:T(8,128)S(1)} %copy-done.37) | data formatting | bytes 786432 | tf_op jit(solution)/shard_map/reduce_sum | solution.py:99
  364.5 5.7 reduce_sum.133
  370.3 24.5 %all-gather.1 = f32[512,96]{1,0:T(8,128)S(1)} all-gather(f32[64,96]{1,0:T(8,128)S(1)} %broadcast_multiply_fusion.1), channel_id=3, replica_groups=mesh['tm'=4,'space'=8] {'space'}, dimensions={0}, use_global_device_ids=true | all-gather | bytes 221184 | tf_op jit(solution)/shard_map/all_gather | solution.py:140
  400.2 14.7 %fusion.44 = f32[]{:T(128)} fusion(f32[6,258,386]{2,1,0:T(8,128)S(1)} %select_maximum_fusion, f32[1,256,384]{2,1,0:T(8,128)} %copy-done.27, f32[4,256,384]{2,1,0:T(8,128)} %copy-done.20, f32[1,256,384]{2,1,0:T(8,128)} %collective-permute-done.11, f32[4,256,384]{2,1,0:T(8,128)} %get-tuple-element.308, f32[]{:T(128)S(6)} %div.85, ...), kind=kLoop, calls=%fused_computation.83 | loop fusion | flops 31850496 | bytes 44826668 | tf_op jit(solution)/shard_map/reduce_sum | solution.py:67
  417.4 16.9 %psum.63 = f32[]{:T(128)} all-reduce(f32[]{:T(128)} %fusion.44), channel_id=1, replica_groups=mesh['tm'=4,'space'=8] {'space'}, use_global_device_ids=true, to_apply=%region_15.16 | all-reduce | flops 1 | bytes 8 | tf_op jit(solution)/shard_map/psum | solution.py:67
  435.5 3.5 fusion.287
  439.1 14.6 %reduce_sum.135 = f32[64,4,96,4]{3,2,1,0:T(8,128)} reshape(f32[256,384]{1,0:T(8,128)S(1)} %get-tuple-element.304) | data formatting | bytes 786432 | tf_op jit(solution)/shard_map/reduce_sum | solution.py:99
  453.7 5.8 reduce_sum.136
  459.6 24.5 %all-gather.2 = f32[512,96]{1,0:T(8,128)S(1)} all-gather(f32[64,96]{1,0:T(8,128)S(1)} %broadcast_multiply_fusion), channel_id=4, replica_groups=mesh['tm'=4,'space'=8] {'space'}, dimensions={0}, use_global_device_ids=true | all-gather | bytes 221184 | tf_op jit(solution)/shard_map/all_gather | solution.py:148
  484.5 62.8 %while.15 = (s32[]{:T(128)}, f32[8,64,96]{2,1,0:T(8,128)S(1)}, s32[]{:T(128)}, f32[8,64,96]{2,1,0:T(8,128)S(1)}, f32[8,64,96]{2,1,0:T(8,128)S(1)}, /*index=5*/f3...) while((s32[]{:T(128)}, f32[8,64,96]{2,1,0:T(8,128)S(1)}, ...), condition=%wide.region_23.24_spmd, body=%wide.region_22.23_spmd.sunk | while | flops 2015235 | bytes 7274663 | solution.py:158
  485.3 41.5 %collective-permute-start = (f32[8,64,96]{2,1,0:T(8,128)S(1)}, f32[8,64,96]{2,1,0:T(8,128)S(1)}, u32[]{:S(2)}, u32[]{:S(2)}) collective-permute-start(f32[8,64,96]{2,1,0:T(8,128)S(1)} %fusion.304), channel_id=1, source_target_pairs={{0,8},{8,16},{16,24},{1,9},{9,17},{17,25},{2,10},{10,18},{18,26},{... | collective-permute-start | bytes 589832 | tf_op jit(solution)/shard_map/while/body/eval_jaxpr/ppermute | solution.py:31
  526.8 3.3 collective-permute-done
  530.9 4.4 collective-permute-start
  535.4 3.3 collective-permute-done
  539.5 4.4 collective-permute-start
  543.9 3.3 collective-permute-done
  548.2 5.5 broadcast_in_dim.72
  553.8 11.8 %broadcast_in_dim.73 = f32[256,384]{1,0:T(8,128)S(1)} reshape(f32[64,4,96,4]{3,2,1,0:T(8,128)} %broadcast_in_dim.72) | data formatting | bytes 786432 | tf_op jit(solution)/shard_map/broadcast_in_dim | solution.py:104
  565.7 4.5 collective-permute-start.13
  570.2 17.3 %collective-permute-done.13 = f32[4,256,384]{2,1,0:T(8,128)S(1)} collective-permute-done((f32[4,256,384]{2,1,0:T(8,128)S(1)}, f32[4,256,384]{2,1,0:T(8,128)S(1)}, u32[]{:S(2)}, u32[]{:S(2)}) %collective-permute-start.13) | collective-permute-done | bytes 1572896 | tf_op jit(solution)/shard_map/ppermute | solution.py:31
  (136 shorter events, 50.0 us)
Async XLA Ops:
  10.7 22.2 %copy-start.22 = (f32[4,256,384]{2,1,0:T(8,128)}, f32[4,256,384]{2,1,0:T(8,128)S(1)}, u32[]{:S(2)}) copy-start(f32[4,256,384]{2,1,0:T(8,128)S(1)} %bitcast_multiply_fusion) | copy-start | bytes 4718596
  10.7 12.8 %collective-permute-start.2 = (f32[1,256,384]{2,1,0:T(8,128)S(1)}, f32[1,256,384]{2,1,0:T(8,128)S(1)}, u32[]{:S(2)}, u32[]{:S(2)}) collective-permute-start(f32[1,256,384]{2,1,0:T(8,128)S(1)} %get-tuple-element.327), channel_id=1, source_target_pairs={{1,0},{2,1},{3,2},{4,3},{5,4},{6,5},{7,6},{9,8},{10,9},{11,10},{12... | collective-permute-start | bytes 1179656 | tf_op jit(solution)/shard_map/ppermute | solution.py:23
  12.0 20.8 %collective-permute-start.1 = (f32[1,256,384]{2,1,0:T(8,128)S(1)}, f32[1,256,384]{2,1,0:T(8,128)S(1)}, u32[]{:S(2)}, u32[]{:S(2)}) collective-permute-start(f32[1,256,384]{2,1,0:T(8,128)S(1)} %get-tuple-element.326), channel_id=1, source_target_pairs={{0,1},{1,2},{2,3},{3,4},{4,5},{5,6},{6,7},{8,9},{9,10},{10,11},{11... | collective-permute-start | bytes 1179656 | tf_op jit(solution)/shard_map/ppermute | solution.py:22
  23.5 9.3 %copy-start.31 = (f32[1,256,384]{2,1,0:T(8,128)}, f32[1,256,384]{2,1,0:T(8,128)S(1)}, u32[]{:S(2)}) copy-start(f32[1,256,384]{2,1,0:T(8,128)S(1)} %collective-permute-done.2) | copy-start | bytes 1179652
  49.5 23.6 %copy-start.18 = (f32[4,256,384]{2,1,0:T(8,128)S(1)}, f32[4,256,384]{2,1,0:T(8,128)}, u32[]{:S(2)}) copy-start(f32[4,256,384]{2,1,0:T(8,128)} %get-tuple-element.312) | copy-start | bytes 4718596
  50.8 13.2 %collective-permute-start.4 = (f32[1,256,384]{2,1,0:T(8,128)S(1)}, f32[1,256,384]{2,1,0:T(8,128)S(1)}, u32[]{:S(2)}, u32[]{:S(2)}) collective-permute-start(f32[1,256,384]{2,1,0:T(8,128)S(1)} %get-tuple-element.325), channel_id=1, source_target_pairs={{1,0},{2,1},{3,2},{4,3},{5,4},{6,5},{7,6},{9,8},{10,9},{11,10},{12... | collective-permute-start | bytes 1179656 | tf_op jit(solution)/shard_map/ppermute | solution.py:23
  52.1 21.0 %collective-permute-start.3 = (f32[1,256,384]{2,1,0:T(8,128)S(1)}, f32[1,256,384]{2,1,0:T(8,128)S(1)}, u32[]{:S(2)}, u32[]{:S(2)}) collective-permute-start(f32[1,256,384]{2,1,0:T(8,128)S(1)} %get-tuple-element.324), channel_id=1, source_target_pairs={{0,1},{1,2},{2,3},{3,4},{4,5},{5,6},{6,7},{8,9},{9,10},{10,11},{11... | collective-permute-start | bytes 1179656 | tf_op jit(solution)/shard_map/ppermute | solution.py:22
  63.9 10.1 %copy-start.29 = (f32[1,256,384]{2,1,0:T(8,128)}, f32[1,256,384]{2,1,0:T(8,128)S(1)}, u32[]{:S(2)}) copy-start(f32[1,256,384]{2,1,0:T(8,128)S(1)} %collective-permute-done.4) | copy-start | bytes 1179652
  107.6 18.8 %copy-start = (s32[4,256,384]{2,1,0:T(8,128)S(1)}, s32[4,256,384]{2,1,0:T(8,128)}, u32[]{:S(2)}) copy-start(s32[4,256,384]{2,1,0:T(8,128)} %param.6) | copy-start | bytes 4718596
  107.6 18.8 %copy-start.13 = (f32[4,256,384]{2,1,0:T(8,128)S(1)}, f32[4,256,384]{2,1,0:T(8,128)}, u32[]{:S(2)}) copy-start(f32[4,256,384]{2,1,0:T(8,128)} %get-tuple-element.313) | copy-start | bytes 4718596
  134.5 17.7 %copy-start.23 = (f32[4,256,384]{2,1,0:T(8,128)}, f32[4,256,384]{2,1,0:T(8,128)S(1)}, u32[]{:S(2)}) copy-start(f32[4,256,384]{2,1,0:T(8,128)S(1)} %sqrt_multiply_fusion.3) | copy-start | bytes 4718596
  134.6 8.7 %collective-permute-start.6 = (f32[1,256,384]{2,1,0:T(8,128)S(1)}, f32[1,256,384]{2,1,0:T(8,128)S(1)}, u32[]{:S(2)}, u32[]{:S(2)}) collective-permute-start(f32[1,256,384]{2,1,0:T(8,128)S(1)} %get-tuple-element.323), channel_id=1, source_target_pairs={{1,0},{2,1},{3,2},{4,3},{5,4},{6,5},{7,6},{9,8},{10,9},{11,10},{12... | collective-permute-start | bytes 1179656 | tf_op jit(solution)/shard_map/ppermute | solution.py:23
  135.9 16.4 %collective-permute-start.5 = (f32[1,256,384]{2,1,0:T(8,128)S(1)}, f32[1,256,384]{2,1,0:T(8,128)S(1)}, u32[]{:S(2)}, u32[]{:S(2)}) collective-permute-start(f32[1,256,384]{2,1,0:T(8,128)S(1)} %get-tuple-element.322), channel_id=1, source_target_pairs={{0,1},{1,2},{2,3},{3,4},{4,5},{5,6},{6,7},{8,9},{9,10},{10,11},{11... | collective-permute-start | bytes 1179656 | tf_op jit(solution)/shard_map/ppermute | solution.py:22
  143.3 9.0 %copy-start.33 = (f32[1,256,384]{2,1,0:T(8,128)}, f32[1,256,384]{2,1,0:T(8,128)S(1)}, u32[]{:S(2)}) copy-start(f32[1,256,384]{2,1,0:T(8,128)S(1)} %collective-permute-done.6) | copy-start | bytes 1179652
  197.6 11.9 %copy-start.19 = (f32[4,256,384]{2,1,0:T(8,128)}, f32[4,256,384]{2,1,0:T(8,128)S(1)}, u32[]{:S(2)}) copy-start(f32[4,256,384]{2,1,0:T(8,128)S(1)} %get-tuple-element.309) | copy-start | bytes 4718596
  197.6 8.5 %collective-permute-start.8 = (f32[1,256,384]{2,1,0:T(8,128)S(1)}, f32[1,256,384]{2,1,0:T(8,128)S(1)}, u32[]{:S(2)}, u32[]{:S(2)}) collective-permute-start(f32[1,256,384]{2,1,0:T(8,128)S(1)} %get-tuple-element.321), channel_id=1, source_target_pairs={{1,0},{2,1},{3,2},{4,3},{5,4},{6,5},{7,6},{9,8},{10,9},{11,10},{12... | collective-permute-start | bytes 1179656 | tf_op jit(solution)/shard_map/ppermute | solution.py:23
  198.9 9.5 %collective-permute-start.7 = (f32[1,256,384]{2,1,0:T(8,128)S(1)}, f32[1,256,384]{2,1,0:T(8,128)S(1)}, u32[]{:S(2)}, u32[]{:S(2)}) collective-permute-start(f32[1,256,384]{2,1,0:T(8,128)S(1)} %get-tuple-element.320), channel_id=1, source_target_pairs={{0,1},{1,2},{2,3},{3,4},{4,5},{5,6},{6,7},{8,9},{9,10},{10,11},{11... | collective-permute-start | bytes 1179656 | tf_op jit(solution)/shard_map/ppermute | solution.py:22
  206.1 3.3 copy-start.30
  224.4 7.8 %copy-start.16 = (f32[1,4,256,384]{3,2,1,0:T(8,128)S(1)}, f32[1,4,256,384]{3,2,1,0:T(8,128)}, u32[]{:S(2)}) copy-start(f32[1,4,256,384]{3,2,1,0:T(8,128)} %param.5) | copy-start | bytes 4718596
  225.7 51.9 %collective-permute-start.10 = (f32[1,256,384]{2,1,0:T(8,128)S(1)}, f32[1,256,384]{2,1,0:T(8,128)S(1)}, u32[]{:S(2)}, u32[]{:S(2)}) collective-permute-start(f32[1,256,384]{2,1,0:T(8,128)S(1)} %get-tuple-element.319), channel_id=1, source_target_pairs={{1,0},{2,1},{3,2},{4,3},{5,4},{6,5},{7,6},{9,8},{10,9},{11,10},{12... | collective-permute-start | bytes 1179656 | tf_op jit(solution)/shard_map/ppermute | solution.py:23
  227.0 51.4 %collective-permute-start.9 = (f32[1,256,384]{2,1,0:T(8,128)S(1)}, f32[1,256,384]{2,1,0:T(8,128)}, u32[]{:S(2)}, u32[]{:S(2)}) collective-permute-start(f32[1,256,384]{2,1,0:T(8,128)S(1)} %get-tuple-element.318), channel_id=1, source_target_pairs={{0,1},{1,2},{2,3},{3,4},{4,5},{5,6},{6,7},{8,9},{9,10},{10,11},{11... | collective-permute-start | bytes 1179656 | tf_op jit(solution)/shard_map/ppermute | solution.py:22
  277.6 118.5 %copy-start.25 = (f32[512,96]{1,0:T(8,128)}, f32[512,96]{1,0:T(8,128)S(1)}, u32[]{:S(2)}) copy-start(f32[512,96]{1,0:T(8,128)S(1)} %all-gather) | copy-start | bytes 589828
  314.6 19.1 %copy-start.1 = (s32[4,256,384]{2,1,0:T(8,128)S(1)}, s32[4,256,384]{2,1,0:T(8,128)}, u32[]{:S(2)}) copy-start(s32[4,256,384]{2,1,0:T(8,128)} %param.6) | copy-start | bytes 4718596
  314.6 19.1 %copy-start.14 = (f32[4,256,384]{2,1,0:T(8,128)S(1)}, f32[4,256,384]{2,1,0:T(8,128)}, u32[]{:S(2)}) copy-start(f32[4,256,384]{2,1,0:T(8,128)} %get-tuple-element.308) | copy-start | bytes 4718596
  342.6 1.1 copy-start.20
  342.6 7.2 %copy-start.37 = (f32[256,384]{1,0:T(8,128)S(1)}, f32[256,384]{1,0:T(8,128)}, u32[]{:S(2)}) copy-start(f32[256,384]{1,0:T(8,128)} %get-tuple-element.314) | copy-start | bytes 1179652
  343.8 53.3 %collective-permute-start.12 = (f32[1,256,384]{2,1,0:T(8,128)S(1)}, f32[1,256,384]{2,1,0:T(8,128)S(1)}, u32[]{:S(2)}, u32[]{:S(2)}) collective-permute-start(f32[1,256,384]{2,1,0:T(8,128)S(1)} %get-tuple-element.317), channel_id=1, source_target_pairs={{1,0},{2,1},{3,2},{4,3},{5,4},{6,5},{7,6},{9,8},{10,9},{11,10},{12... | collective-permute-start | bytes 1179656 | tf_op jit(solution)/shard_map/ppermute | solution.py:23
  345.1 52.8 %collective-permute-start.11 = (f32[1,256,384]{2,1,0:T(8,128)S(1)}, f32[1,256,384]{2,1,0:T(8,128)}, u32[]{:S(2)}, u32[]{:S(2)}) collective-permute-start(f32[1,256,384]{2,1,0:T(8,128)S(1)} %get-tuple-element.316), channel_id=1, source_target_pairs={{0,1},{1,2},{2,3},{3,4},{4,5},{5,6},{6,7},{8,9},{9,10},{10,11},{11... | collective-permute-start | bytes 1179656 | tf_op jit(solution)/shard_map/ppermute | solution.py:22
  396.1 1.0 copy-start.4
  396.1 1.0 copy-start.6
  396.1 1.1 copy-start.8
  396.1 1.1 copy-start.10
  396.1 2.0 copy-start.21
  415.0 20.6 %copy-start.15 = (f32[4,256,384]{2,1,0:T(8,128)S(1)}, f32[4,256,384]{2,1,0:T(8,128)}, u32[]{:S(2)}) copy-start(f32[4,256,384]{2,1,0:T(8,128)} %get-tuple-element.308) | copy-start | bytes 4718596
  453.7 30.4 %copy-start.3 = (f32[8,64,96]{2,1,0:T(8,128)S(1)}, f32[8,64,96]{2,1,0:T(8,128)}, u32[]{:S(2)}) copy-start(f32[8,64,96]{2,1,0:T(8,128)} %copy-done.2) | copy-start | bytes 589828
  453.7 30.4 %copy-start.5 = (f32[8,64,96]{2,1,0:T(8,128)S(1)}, f32[8,64,96]{2,1,0:T(8,128)}, u32[]{:S(2)}) copy-start(f32[8,64,96]{2,1,0:T(8,128)} %copy-done.4) | copy-start | bytes 589828
  453.7 30.4 %copy-start.7 = (f32[8,64,96]{2,1,0:T(8,128)S(1)}, f32[8,64,96]{2,1,0:T(8,128)}, u32[]{:S(2)}) copy-start(f32[8,64,96]{2,1,0:T(8,128)} %copy-done.6) | copy-start | bytes 589828
  453.7 30.4 %copy-start.9 = (f32[8,64,96]{2,1,0:T(8,128)S(1)}, f32[8,64,96]{2,1,0:T(8,128)}, u32[]{:S(2)}) copy-start(f32[8,64,96]{2,1,0:T(8,128)} %copy-done.8) | copy-start | bytes 589828
  453.7 30.4 %copy-start.11 = (f32[8,64,96]{2,1,0:T(8,128)S(1)}, f32[8,64,96]{2,1,0:T(8,128)}, u32[]{:S(2)}) copy-start(f32[8,64,96]{2,1,0:T(8,128)} %copy-done.10) | copy-start | bytes 589828
  453.7 30.4 %copy-start.26 = (f32[512,96]{1,0:T(8,128)S(1)}, f32[512,96]{1,0:T(8,128)}, u32[]{:S(2)}) copy-start(f32[512,96]{1,0:T(8,128)} %copy-done.25) | copy-start | bytes 589828
  459.6 24.9 %copy-start.12 = (f32[8,64,96]{2,1,0:T(8,128)S(1)}, f32[8,64,96]{2,1,0:T(8,128)}, u32[]{:S(2)}) copy-start(f32[8,64,96]{2,1,0:T(8,128)} %get-tuple-element.420) | copy-start | bytes 589828
  485.3 44.8 %collective-permute-start = (f32[8,64,96]{2,1,0:T(8,128)S(1)}, f32[8,64,96]{2,1,0:T(8,128)S(1)}, u32[]{:S(2)}, u32[]{:S(2)}) collective-permute-start(f32[8,64,96]{2,1,0:T(8,128)S(1)} %fusion.304), channel_id=1, source_target_pairs={{0,8},{8,16},{16,24},{1,9},{9,17},{17,25},{2,10},{10,18},{18,26},{... | collective-permute-start | bytes 589832 | tf_op jit(solution)/shard_map/while/body/eval_jaxpr/ppermute | solution.py:31
  530.9 7.7 %collective-permute-start = (f32[8,64,96]{2,1,0:T(8,128)S(1)}, f32[8,64,96]{2,1,0:T(8,128)S(1)}, u32[]{:S(2)}, u32[]{:S(2)}) collective-permute-start(f32[8,64,96]{2,1,0:T(8,128)S(1)} %fusion.304), channel_id=1, source_target_pairs={{0,8},{8,16},{16,24},{1,9},{9,17},{17,25},{2,10},{10,18},{18,26},{... | collective-permute-start | bytes 589832 | tf_op jit(solution)/shard_map/while/body/eval_jaxpr/ppermute | solution.py:31
  539.5 7.7 %collective-permute-start = (f32[8,64,96]{2,1,0:T(8,128)S(1)}, f32[8,64,96]{2,1,0:T(8,128)S(1)}, u32[]{:S(2)}, u32[]{:S(2)}) collective-permute-start(f32[8,64,96]{2,1,0:T(8,128)S(1)} %fusion.304), channel_id=1, source_target_pairs={{0,8},{8,16},{16,24},{1,9},{9,17},{17,25},{2,10},{10,18},{18,26},{... | collective-permute-start | bytes 589832 | tf_op jit(solution)/shard_map/while/body/eval_jaxpr/ppermute | solution.py:31
  548.2 5.6 copy-start.38
  553.8 11.8 %copy-start.24 = (f32[4,256,384]{2,1,0:T(8,128)S(1)}, f32[4,256,384]{2,1,0:T(8,128)}, u32[]{:S(2)}) copy-start(f32[4,256,384]{2,1,0:T(8,128)} %get-tuple-element.305) | copy-start | bytes 4718596
  565.6 22.0 %copy-start.17 = (f32[1,4,256,384]{3,2,1,0:T(8,128)S(1)}, f32[1,4,256,384]{3,2,1,0:T(8,128)}, u32[]{:S(2)}) copy-start(f32[1,4,256,384]{3,2,1,0:T(8,128)} %param.5) | copy-start | bytes 4718596
  565.7 21.9 %collective-permute-start.13 = (f32[4,256,384]{2,1,0:T(8,128)S(1)}, f32[4,256,384]{2,1,0:T(8,128)S(1)}, u32[]{:S(2)}, u32[]{:S(2)}) collective-permute-start(f32[4,256,384]{2,1,0:T(8,128)S(1)} %broadcast_add_fusion), channel_id=1, source_target_pairs={{0,8},{8,16},{16,24},{1,9},{9,17},{17,25},{2,10},{10,18},{18,26},{... | collective-permute-start | bytes 4718600 | tf_op jit(solution)/shard_map/ppermute | solution.py:31
  (7 other events, 6.1 us)
where the time goes:
time: 598 us; the launch traced here: 589 us
  other arithmetic  172 us (29%)
  blocking collectives  171 us (29%)
  starting transfers between devices  90.2 us (15%)
  waiting for transfers between devices  77.1 us (13%)
  local copies, waits for them, and re-layouts  70.3 us (12%)
  between operations  9.11 us (2%)
    psum x4, blocking collectives, grid_squares(): return lax.psum(jnp.sum(resid * resid), 'space')  63.1 us
    reduce_sum x4, other arithmetic, grid_curvature(): return lax.psum(jnp.sum(direction * image), 'space')  60.1 us
    mul x5, other arithmetic, operate(): scaled = root_cond * vector  57.2 us
    ppermute x4, starting transfers between devices, shifted(): return lax.ppermute(x, axis, pairs)  54.8 us
    reduce_sum x3, local copies, waits for them, and re-layouts, restrict(): return jnp.mean(blocks, axis=(1, 3, 5))  43.9 us
    psum x2, blocking collectives, grid_curvature(): return lax.psum(jnp.sum(direction * image), 'space')  33.5 us
    reduce_sum x6, other arithmetic, restrict(): return jnp.mean(blocks, axis=(1, 3, 5))  29.9 us
    ppermute x6, waiting for transfers between devices, extended(): before = lax.ppermute(last, axis, up)  29.7 us
  transfers between devices with their start and end apart: 16, of which 12 were waited for; matrix products, arithmetic and copies ran while one was open for 7% of the time, Pallas kernels for 0%

commit v1 on v0

--- a/solution.py
+++ b/solution.py
@@ -145,7 +145,26 @@
     tm_index = lax.axis_index("tm")
     slice_count = lax.axis_size("tm")
     local_end = restrict(fine_end)
-    coarse_end = lax.all_gather(local_end, "space", axis=0, tiled=True)
+    long_array, a_now, everything = (
+        lax.axis_size("space"),
+        lax.axis_index("space"),
+        local_end.shape[0],
+    )
+    val2, b_next = (local_end, 1)
+    while b_next < long_array:
+        val2 = jnp.concatenate(
+            [
+                val2,
+                lax.ppermute(
+                    val2,
+                    "space",
+                    [(hop_no, (hop_no - b_next) % long_array) for hop_no in range(long_array)],
+                ),
+            ],
+            axis=0,
+        )
+        b_next = 2 * b_next
+    coarse_end = jnp.roll(val2, a_now * everything, 0)
     jump_term = coarse_end - coarse_old
     coarse_rows = local_end.shape[0]
     carry_start = jnp.where(tm_index == 0, coarse_start, jnp.zeros_like(coarse_start))

time: 598 us -> 583 us (0.975)
  blocking collectives: 171 us -> 150 us
    all_gather x1 -> x0, blocking collectives: 24.5 us -> none  [local(): coarse_end = lax.all_gather(local_end, 'space', axis=0, tiled=True)]
    ppermute x6, waiting for transfers between devices: 20.2 us -> 0.02 us  [extended(): after = lax.ppermute(leading, axis, down)]
    ppermute x6, waiting for transfers between devices: 29.7 us -> 43.8 us  [extended(): before = lax.ppermute(last, axis, up)]
    ppermute x0 -> x3, waiting for transfers between devices: none -> 11.2 us  [local(): lax.ppermute(val2, 'space', [(hop_no, (hop_no - b_next) % long_array) for...]
  transfers between devices with their start and end apart: 16 -> 19, of which waited for: 12 -> 11; matrix products, arithmetic and copies ran while one was open for 7% -> 8% of each run, Pallas kernels for 0% -> 0%
where the time goes in v1:
time: 583 us; the launch traced here: 574 us
  other arithmetic  172 us (30%)
  blocking collectives  150 us (26%)
  starting transfers between devices  87.1 us (15%)
  waiting for transfers between devices  82.2 us (14%)
  local copies, waits for them, and re-layouts  72.4 us (12%)
  between operations  9.25 us (2%)
    psum x4, blocking collectives, grid_squares(): return lax.psum(jnp.sum(resid * resid), 'space')  66.6 us
    reduce_sum x4, other arithmetic, grid_curvature(): return lax.psum(jnp.sum(direction * image), 'space')  60.5 us
    mul x5, other arithmetic, operate(): scaled = root_cond * vector  57.5 us
    ppermute x4, starting transfers between devices, shifted(): return lax.ppermute(x, axis, pairs)  55.1 us
    reduce_sum x3, local copies, waits for them, and re-layouts, restrict(): return jnp.mean(blocks, axis=(1, 3, 5))  44 us
    ppermute x6, waiting for transfers between devices, extended(): before = lax.ppermute(last, axis, up)  43.8 us
    psum x2, blocking collectives, grid_curvature(): return lax.psum(jnp.sum(direction * image), 'space')  32.6 us
    reduce_sum x6, other arithmetic, restrict(): return jnp.mean(blocks, axis=(1, 3, 5))  29.9 us
  transfers between devices with their start and end apart: 19, of which 11 were waited for; matrix products, arithmetic and copies ran while one was open for 8% of the time, Pallas kernels for 0%

profile of v1, /device:TPU:1, one launch (start us, length us, event | category | flops | bytes accessed | tf_op | source)
XLA Modules:
  0.0 573.8 jit_solution(4308228425982850501)
XLA Ops:
  2.2 8.5 %bitcast_multiply_fusion = f32[4,256,384]{2,1,0:T(8,128)S(1)} fusion(f32[1,4,256,384]{3,2,1,0:T(8,128)} %param.5, f32[]{:T(128)} %bitcast.8, s32[4,256,384]{2,1,0:T(8,128)} %param.6, f32[]{:T(128)} %bitcast.7, f32[]{:T(128)} %bitcast.6, f32[]{:T(128)} %bitcast.5, f32[]{:T(128)} %bitcast.4, f32[]{:T(128)} %bitcast.3, f32[]{:T(128)} %bitcast.2, f32[]{:T(128)} %bitcast.1), kind=kLoop, calls=%fused_computation.382 | loop fusion | flops 9437184 | bytes 4718624 | tf_op jit(solution)/shard_map/mul | solution.py:56
  10.8 4.0 collective-permute-start.1
  16.1 14.9 %collective-permute-done.1 = f32[1,256,384]{2,1,0:T(8,128)S(1)} collective-permute-done((f32[1,256,384]{2,1,0:T(8,128)S(1)}, f32[1,256,384]{2,1,0:T(8,128)S(1)}, u32[]{:S(2)}, u32[]{:S(2)}) %collective-permute-start.1) | collective-permute-done | bytes 393248 | tf_op jit(solution)/shard_map/ppermute | solution.py:22
  33.5 15.0 %sqrt_multiply_fusion.4 = (f32[4,256,384]{2,1,0:T(8,128)}, f32[4,256,384]{2,1,0:T(8,128)}) fusion(f32[]{:T(128)} %bitcast.8, s32[4,256,384]{2,1,0:T(8,128)} %param.6, f32[]{:T(128)} %bitcast.7, f32[]{:T(128)} %bitcast.6, f32[]{:T(128)} %bitcast.5, f32[]{:T(128)} %bitcast.4, f32[]{:T(128)} %bitcast.3, f32[]{:T(128)} %bitcast.2, f32[]{:T(128)} %bitcast.1, ...), kind=kLoop, calls=%fused_computation.402 | loop fusion | flops 30277632 | bytes 46399520 | tf_op jit(solution)/shard_map/mul | solution.py:56
  49.7 4.1 collective-permute-start.3
  55.2 13.9 %collective-permute-done.3 = f32[1,256,384]{2,1,0:T(8,128)S(1)} collective-permute-done((f32[1,256,384]{2,1,0:T(8,128)S(1)}, f32[1,256,384]{2,1,0:T(8,128)S(1)}, u32[]{:S(2)}, u32[]{:S(2)}) %collective-permute-start.3) | collective-permute-done | bytes 393248 | tf_op jit(solution)/shard_map/ppermute | solution.py:22
  70.2 15.4 %multiply_reduce_fusion.4 = (f32[]{:T(128)}, f32[]{:T(128)}, f32[4,256,384]{2,1,0:T(8,128)}) fusion(f32[4,256,384]{2,1,0:T(8,128)} %get-tuple-element.313, f32[6,258,386]{2,1,0:T(8,128)S(1)} %select_maximum_fusion.8, f32[1,256,384]{2,1,0:T(8,128)} %copy-done.32, f32[4,256,384]{2,1,0:T(8,128)} %get-tuple-element.312, f32[1,256,384]{2,1,0:T(8,128)} %copy-done.29, ...), kind=kLoop, calls=%fused_computation.394 | loop fusion | flops 31064064 | bytes 44826664 | tf_op jit(solution)/shard_map/reduce_sum | solution.py:67
  85.6 21.7 %all-reduce.16 = (f32[]{:T(128)}, f32[]{:T(128)}) all-reduce(f32[]{:T(128)} %get-tuple-element.270, f32[]{:T(128)} %get-tuple-element.269), channel_id=1, replica_groups=mesh['tm'=4,'space'=8] {'space'}, use_global_device_ids=true, to_apply=%region_1.2 | all-reduce | flops 2 | bytes 16 | tf_op jit(solution)/shard_map/psum | solution.py:63
  111.7 14.4 %psum.58 = f32[]{:T(128)} all-reduce(f32[]{:T(128)} %multiply_reduce_fusion.3), channel_id=1, replica_groups=mesh['tm'=4,'space'=8] {'space'}, use_global_device_ids=true, to_apply=%region_5.6 | all-reduce | flops 1 | bytes 8 | tf_op jit(solution)/shard_map/psum | solution.py:63
  127.4 8.2 %sqrt_multiply_fusion.3 = f32[4,256,384]{2,1,0:T(8,128)S(1)} fusion(f32[4,256,384]{2,1,0:T(8,128)S(1)} %copy-done.13, f32[]{:T(128)S(6)} %div.82, f32[4,256,384]{2,1,0:T(8,128)} %get-tuple-element.311, f32[]{:T(128)S(6)} %div.81, f32[]{:T(128)} %bitcast.8, s32[4,256,384]{2,1,0:T(8,128)S(1)} %copy-done, f32[]{:T(128)} %bitcast.7, f32[]{:T(128)} %bitcast.6, ...), kind=kLoop, calls=%fused_computation.401 | loop fusion | flops 11010048 | bytes 6291496 | tf_op jit(solution)/shard_map/mul | solution.py:56
  135.7 3.5 collective-permute-start.5
  140.5 7.6 %collective-permute-done.5 = f32[1,256,384]{2,1,0:T(8,128)S(1)} collective-permute-done((f32[1,256,384]{2,1,0:T(8,128)S(1)}, f32[1,256,384]{2,1,0:T(8,128)S(1)}, u32[]{:S(2)}, u32[]{:S(2)}) %collective-permute-start.5) | collective-permute-done | bytes 393248 | tf_op jit(solution)/shard_map/ppermute | solution.py:22
  150.7 14.9 %fusion.43 = f32[]{:T(128)} fusion(f32[6,258,386]{2,1,0:T(8,128)S(1)} %select_maximum_fusion.6, f32[1,256,384]{2,1,0:T(8,128)} %copy-done.36, f32[4,256,384]{2,1,0:T(8,128)} %copy-done.23, f32[1,256,384]{2,1,0:T(8,128)} %copy-done.33, f32[4,256,384]{2,1,0:T(8,128)} %get-tuple-element.313, f32[]{:T(128)S(6)} %div.82, f32[4,256,384]{2,1,0:T(8,128)} %get-tuple-element.311, ...), kind=kLoop, calls=%fused_computation.82 | loop fusion | flops 31850496 | bytes 44826668 | tf_op jit(solution)/shard_map/reduce_sum | solution.py:67
  165.6 17.0 %psum.59 = f32[]{:T(128)} all-reduce(f32[]{:T(128)} %fusion.43), channel_id=1, replica_groups=mesh['tm'=4,'space'=8] {'space'}, use_global_device_ids=true, to_apply=%region_7.8 | all-reduce | flops 1 | bytes 8 | tf_op jit(solution)/shard_map/psum | solution.py:67
  183.8 11.0 %sqrt_multiply_fusion.2 = (f32[4,256,384]{2,1,0:T(8,128)S(1)}, f32[4,256,384]{2,1,0:T(8,128)}) fusion(f32[]{:T(128)} %bitcast.8, s32[4,256,384]{2,1,0:T(8,128)} %param.6, f32[]{:T(128)} %bitcast.7, f32[]{:T(128)} %bitcast.6, f32[]{:T(128)} %bitcast.5, f32[]{:T(128)} %bitcast.4, f32[]{:T(128)} %bitcast.3, f32[]{:T(128)} %bitcast.2, f32[]{:T(128)} %bitcast.1, ...), kind=kLoop, calls=%fused_computation.400 | loop fusion | flops 12582912 | bytes 9437228 | tf_op jit(solution)/shard_map/mul | solution.py:56
  194.8 3.7 collective-permute-start.7
  200.0 7.4 %collective-permute-done.7 = f32[1,256,384]{2,1,0:T(8,128)S(1)} collective-permute-done((f32[1,256,384]{2,1,0:T(8,128)S(1)}, f32[1,256,384]{2,1,0:T(8,128)S(1)}, u32[]{:S(2)}, u32[]{:S(2)}) %collective-permute-start.7) | collective-permute-done | bytes 393248 | tf_op jit(solution)/shard_map/ppermute | solution.py:22
  208.4 14.9 %sqrt_multiply_fusion.1 = (f32[4,256,384]{2,1,0:T(8,128)}, f32[4,256,384]{2,1,0:T(8,128)}) fusion(f32[]{:T(128)} %bitcast.8, s32[4,256,384]{2,1,0:T(8,128)} %param.6, f32[]{:T(128)} %bitcast.7, f32[]{:T(128)} %bitcast.6, f32[]{:T(128)} %bitcast.5, f32[]{:T(128)} %bitcast.4, f32[]{:T(128)} %bitcast.3, f32[]{:T(128)} %bitcast.2, f32[]{:T(128)} %bitcast.1, ...), kind=kLoop, calls=%fused_computation.399 | loop fusion | flops 30277632 | bytes 46399520 | tf_op jit(solution)/shard_map/mul | solution.py:56
  225.9 5.2 collective-permute-start.9
  231.2 14.7 %reduce_sum.129 = f32[64,4,96,4]{3,2,1,0:T(8,128)} reshape(f32[256,384]{1,0:T(8,128)S(1)} %reduce_sum.128) | data formatting | bytes 786432 | tf_op jit(solution)/shard_map/reduce_sum | solution.py:99
  245.9 5.7 reduce_sum.130
  251.6 24.9 %all-gather = f32[512,96]{1,0:T(8,128)S(1)} all-gather(f32[64,96]{1,0:T(8,128)S(1)} %broadcast_multiply_fusion.1), channel_id=2, replica_groups=mesh['tm'=4,'space'=8] {'space'}, dimensions={0}, use_global_device_ids=true | all-gather | bytes 221184 | tf_op jit(solution)/shard_map/all_gather | solution.py:139
  279.9 15.4 %multiply_reduce_fusion.1 = (f32[]{:T(128)}, f32[]{:T(128)}, f32[4,256,384]{2,1,0:T(8,128)}) fusion(f32[4,256,384]{2,1,0:T(8,128)} %get-tuple-element.308, f32[6,258,386]{2,1,0:T(8,128)S(1)} %select_maximum_fusion.2, f32[1,256,384]{2,1,0:T(8,128)} %copy-done.27, f32[4,256,384]{2,1,0:T(8,128)} %get-tuple-element.307, ...), kind=kLoop, calls=%fused_computation.389 | loop fusion | flops 31064064 | bytes 44826664 | tf_op jit(solution)/shard_map/reduce_sum | solution.py:67
  295.3 15.5 %all-reduce.15 = (f32[]{:T(128)}, f32[]{:T(128)}) all-reduce(f32[]{:T(128)} %get-tuple-element.268, f32[]{:T(128)} %get-tuple-element.267), channel_id=1, replica_groups=mesh['tm'=4,'space'=8] {'space'}, use_global_device_ids=true, to_apply=%region_9.10 | all-reduce | flops 2 | bytes 16 | tf_op jit(solution)/shard_map/psum | solution.py:63
  315.2 15.0 %psum.62 = f32[]{:T(128)} all-reduce(f32[]{:T(128)} %multiply_reduce_fusion), channel_id=1, replica_groups=mesh['tm'=4,'space'=8] {'space'}, use_global_device_ids=true, to_apply=%region_13.14 | all-reduce | flops 1 | bytes 8 | tf_op jit(solution)/shard_map/psum | solution.py:63
  331.4 9.0 %fusion.279 = (f32[256,384]{1,0:T(8,128)}, f32[4,256,384]{2,1,0:T(8,128)S(1)}) fusion(f32[]{:T(128)} %bitcast.8, s32[4,256,384]{2,1,0:T(8,128)S(1)} %copy-done.1, f32[]{:T(128)} %bitcast.7, f32[]{:T(128)} %bitcast.6, f32[]{:T(128)} %bitcast.5, f32[]{:T(128)} %bitcast.4, f32[]{:T(128)} %bitcast.3, f32[]{:T(128)} %bitcast.2, f32[]{:T(128)} %bitcast.1, ...), kind=kLoop, calls=%fused_computation.572 | loop fusion | flops 11304960 | bytes 6684712 | tf_op jit(solution)/shard_map/reduce_sum | solution.py:99
  341.7 3.2 collective-permute-start.11
  346.1 14.7 %reduce_sum.132 = f32[64,4,96,4]{3,2,1,0:T(8,128)} reshape(f32[256,384]{1,0:T(8,128)S(1)} %copy-done.37) | data formatting | bytes 786432 | tf_op jit(solution)/shard_map/reduce_sum | solution.py:99
  360.8 5.7 reduce_sum.133
  366.6 26.1 %all-gather.1 = f32[512,96]{1,0:T(8,128)S(1)} all-gather(f32[64,96]{1,0:T(8,128)S(1)} %broadcast_multiply_fusion), channel_id=3, replica_groups=mesh['tm'=4,'space'=8] {'space'}, dimensions={0}, use_global_device_ids=true | all-gather | bytes 221184 | tf_op jit(solution)/shard_map/all_gather | solution.py:140
  398.1 14.8 %fusion.44 = f32[]{:T(128)} fusion(f32[6,258,386]{2,1,0:T(8,128)S(1)} %select_maximum_fusion, f32[1,256,384]{2,1,0:T(8,128)} %collective-permute-done.12, f32[4,256,384]{2,1,0:T(8,128)} %copy-done.20, f32[1,256,384]{2,1,0:T(8,128)} %copy-done.28, f32[4,256,384]{2,1,0:T(8,128)} %get-tuple-element.308, f32[]{:T(128)S(6)} %div.85, ...), kind=kLoop, calls=%fused_computation.83 | loop fusion | flops 31850496 | bytes 44826668 | tf_op jit(solution)/shard_map/reduce_sum | solution.py:67
  415.3 15.7 %psum.63 = f32[]{:T(128)} all-reduce(f32[]{:T(128)} %fusion.44), channel_id=1, replica_groups=mesh['tm'=4,'space'=8] {'space'}, use_global_device_ids=true, to_apply=%region_15.16 | all-reduce | flops 1 | bytes 8 | tf_op jit(solution)/shard_map/psum | solution.py:67
  432.2 3.5 fusion.286
  435.8 14.6 %reduce_sum.135 = f32[64,4,96,4]{3,2,1,0:T(8,128)} reshape(f32[256,384]{1,0:T(8,128)S(1)} %get-tuple-element.304) | data formatting | bytes 786432 | tf_op jit(solution)/shard_map/reduce_sum | solution.py:99
  450.4 5.8 %reduce_sum.136 = f32[64,96]{1,0:T(8,128)S(1)} reduce(f32[64,4,96,4]{3,2,1,0:T(8,128)} %reduce_sum.135, f32[]{:T(128)} %constant.74.clone.1), dimensions={1,3}, to_apply=%region_21.22 | reduce | flops 92160 | bytes 417796 | tf_op jit(solution)/shard_map/reduce_sum | solution.py:99
  459.2 3.1 collective-permute-done.14
  462.4 5.5 collective-permute-done.15
  468.9 63.1 %while.15 = (s32[]{:T(128)}, f32[8,64,96]{2,1,0:T(8,128)S(1)}, s32[]{:T(128)}, f32[8,64,96]{2,1,0:T(8,128)S(1)}, f32[8,64,96]{2,1,0:T(8,128)S(1)}, /*index=5*/f3...) while((s32[]{:T(128)}, f32[8,64,96]{2,1,0:T(8,128)S(1)}, ...), condition=%wide.region_23.24_spmd, body=%wide.region_22.23_spmd.sunk | while | flops 2015235 | bytes 7274663 | solution.py:177
  469.7 41.8 %collective-permute-start = (f32[8,64,96]{2,1,0:T(8,128)S(1)}, f32[8,64,96]{2,1,0:T(8,128)S(1)}, u32[]{:S(2)}, u32[]{:S(2)}) collective-permute-start(f32[8,64,96]{2,1,0:T(8,128)S(1)} %fusion.303), channel_id=1, source_target_pairs={{0,8},{8,16},{16,24},{1,9},{9,17},{17,25},{2,10},{10,18},{18,26},{... | collective-permute-start | bytes 589832 | tf_op jit(solution)/shard_map/while/body/eval_jaxpr/ppermute | solution.py:31
  511.5 3.3 collective-permute-done
  515.7 4.4 collective-permute-start
  520.1 3.3 collective-permute-done
  524.3 4.4 collective-permute-start
  528.7 3.3 collective-permute-done
  532.9 5.5 broadcast_in_dim.72
  538.5 11.8 %broadcast_in_dim.73 = f32[256,384]{1,0:T(8,128)S(1)} reshape(f32[64,4,96,4]{3,2,1,0:T(8,128)} %broadcast_in_dim.72) | data formatting | bytes 786432 | tf_op jit(solution)/shard_map/broadcast_in_dim | solution.py:104
  550.4 4.5 collective-permute-start.16
  554.9 17.3 %collective-permute-done.16 = f32[4,256,384]{2,1,0:T(8,128)S(1)} collective-permute-done((f32[4,256,384]{2,1,0:T(8,128)S(1)}, f32[4,256,384]{2,1,0:T(8,128)S(1)}, u32[]{:S(2)}, u32[]{:S(2)}) %collective-permute-start.16) | collective-permute-done | bytes 1572896 | tf_op jit(solution)/shard_map/ppermute | solution.py:31
  (151 shorter events, 46.7 us)
Async XLA Ops:
  10.7 20.3 %copy-start.22 = (f32[4,256,384]{2,1,0:T(8,128)}, f32[4,256,384]{2,1,0:T(8,128)S(1)}, u32[]{:S(2)}) copy-start(f32[4,256,384]{2,1,0:T(8,128)S(1)} %bitcast_multiply_fusion) | copy-start | bytes 4718596
  10.8 20.2 %collective-permute-start.1 = (f32[1,256,384]{2,1,0:T(8,128)S(1)}, f32[1,256,384]{2,1,0:T(8,128)S(1)}, u32[]{:S(2)}, u32[]{:S(2)}) collective-permute-start(f32[1,256,384]{2,1,0:T(8,128)S(1)} %get-tuple-element.326), channel_id=1, source_target_pairs={{0,1},{1,2},{2,3},{3,4},{4,5},{5,6},{6,7},{8,9},{9,10},{10,11},{11... | collective-permute-start | bytes 1179656 | tf_op jit(solution)/shard_map/ppermute | solution.py:22
  14.8 16.2 %collective-permute-start.2 = (f32[1,256,384]{2,1,0:T(8,128)S(1)}, f32[1,256,384]{2,1,0:T(8,128)S(1)}, u32[]{:S(2)}, u32[]{:S(2)}) collective-permute-start(f32[1,256,384]{2,1,0:T(8,128)S(1)} %get-tuple-element.327), channel_id=1, source_target_pairs={{1,0},{2,1},{3,2},{4,3},{5,4},{6,5},{7,6},{9,8},{10,9},{11,10},{12... | collective-permute-start | bytes 1179656 | tf_op jit(solution)/shard_map/ppermute | solution.py:23
  48.5 20.7 %copy-start.18 = (f32[4,256,384]{2,1,0:T(8,128)S(1)}, f32[4,256,384]{2,1,0:T(8,128)}, u32[]{:S(2)}) copy-start(f32[4,256,384]{2,1,0:T(8,128)} %get-tuple-element.312) | copy-start | bytes 4718596
  49.7 19.4 %collective-permute-start.3 = (f32[1,256,384]{2,1,0:T(8,128)S(1)}, f32[1,256,384]{2,1,0:T(8,128)S(1)}, u32[]{:S(2)}, u32[]{:S(2)}) collective-permute-start(f32[1,256,384]{2,1,0:T(8,128)S(1)} %get-tuple-element.324), channel_id=1, source_target_pairs={{0,1},{1,2},{2,3},{3,4},{4,5},{5,6},{6,7},{8,9},{9,10},{10,11},{11... | collective-permute-start | bytes 1179656 | tf_op jit(solution)/shard_map/ppermute | solution.py:22
  53.9 15.3 %collective-permute-start.4 = (f32[1,256,384]{2,1,0:T(8,128)S(1)}, f32[1,256,384]{2,1,0:T(8,128)S(1)}, u32[]{:S(2)}, u32[]{:S(2)}) collective-permute-start(f32[1,256,384]{2,1,0:T(8,128)S(1)} %get-tuple-element.325), channel_id=1, source_target_pairs={{1,0},{2,1},{3,2},{4,3},{5,4},{6,5},{7,6},{9,8},{10,9},{11,10},{12... | collective-permute-start | bytes 1179656 | tf_op jit(solution)/shard_map/ppermute | solution.py:23
  69.1 1.0 copy-start.32
  108.6 18.8 %copy-start = (s32[4,256,384]{2,1,0:T(8,128)S(1)}, s32[4,256,384]{2,1,0:T(8,128)}, u32[]{:S(2)}) copy-start(s32[4,256,384]{2,1,0:T(8,128)} %param.6) | copy-start | bytes 4718596
  108.6 18.8 %copy-start.13 = (f32[4,256,384]{2,1,0:T(8,128)S(1)}, f32[4,256,384]{2,1,0:T(8,128)}, u32[]{:S(2)}) copy-start(f32[4,256,384]{2,1,0:T(8,128)} %get-tuple-element.313) | copy-start | bytes 4718596
  135.6 12.5 %copy-start.23 = (f32[4,256,384]{2,1,0:T(8,128)}, f32[4,256,384]{2,1,0:T(8,128)S(1)}, u32[]{:S(2)}) copy-start(f32[4,256,384]{2,1,0:T(8,128)S(1)} %sqrt_multiply_fusion.3) | copy-start | bytes 4718596
  135.7 12.4 %collective-permute-start.5 = (f32[1,256,384]{2,1,0:T(8,128)S(1)}, f32[1,256,384]{2,1,0:T(8,128)S(1)}, u32[]{:S(2)}, u32[]{:S(2)}) collective-permute-start(f32[1,256,384]{2,1,0:T(8,128)S(1)} %get-tuple-element.322), channel_id=1, source_target_pairs={{0,1},{1,2},{2,3},{3,4},{4,5},{5,6},{6,7},{8,9},{9,10},{10,11},{11... | collective-permute-start | bytes 1179656 | tf_op jit(solution)/shard_map/ppermute | solution.py:22
  139.2 8.9 %collective-permute-start.6 = (f32[1,256,384]{2,1,0:T(8,128)S(1)}, f32[1,256,384]{2,1,0:T(8,128)S(1)}, u32[]{:S(2)}, u32[]{:S(2)}) collective-permute-start(f32[1,256,384]{2,1,0:T(8,128)S(1)} %get-tuple-element.323), channel_id=1, source_target_pairs={{1,0},{2,1},{3,2},{4,3},{5,4},{6,5},{7,6},{9,8},{10,9},{11,10},{12... | collective-permute-start | bytes 1179656 | tf_op jit(solution)/shard_map/ppermute | solution.py:23
  194.7 13.6 %copy-start.19 = (f32[4,256,384]{2,1,0:T(8,128)}, f32[4,256,384]{2,1,0:T(8,128)S(1)}, u32[]{:S(2)}) copy-start(f32[4,256,384]{2,1,0:T(8,128)S(1)} %get-tuple-element.309) | copy-start | bytes 4718596
  194.8 12.6 %collective-permute-start.7 = (f32[1,256,384]{2,1,0:T(8,128)S(1)}, f32[1,256,384]{2,1,0:T(8,128)S(1)}, u32[]{:S(2)}, u32[]{:S(2)}) collective-permute-start(f32[1,256,384]{2,1,0:T(8,128)S(1)} %get-tuple-element.320), channel_id=1, source_target_pairs={{0,1},{1,2},{2,3},{3,4},{4,5},{5,6},{6,7},{8,9},{9,10},{10,11},{11... | collective-permute-start | bytes 1179656 | tf_op jit(solution)/shard_map/ppermute | solution.py:22
  198.5 8.9 %collective-permute-start.8 = (f32[1,256,384]{2,1,0:T(8,128)S(1)}, f32[1,256,384]{2,1,0:T(8,128)S(1)}, u32[]{:S(2)}, u32[]{:S(2)}) collective-permute-start(f32[1,256,384]{2,1,0:T(8,128)S(1)} %get-tuple-element.321), channel_id=1, source_target_pairs={{1,0},{2,1},{3,2},{4,3},{5,4},{6,5},{7,6},{9,8},{10,9},{11,10},{12... | collective-permute-start | bytes 1179656 | tf_op jit(solution)/shard_map/ppermute | solution.py:23
  223.3 7.8 %copy-start.16 = (f32[1,4,256,384]{3,2,1,0:T(8,128)S(1)}, f32[1,4,256,384]{3,2,1,0:T(8,128)}, u32[]{:S(2)}) copy-start(f32[1,4,256,384]{3,2,1,0:T(8,128)} %param.5) | copy-start | bytes 4718596
  224.6 51.9 %collective-permute-start.10 = (f32[1,256,384]{2,1,0:T(8,128)S(1)}, f32[1,256,384]{2,1,0:T(8,128)S(1)}, u32[]{:S(2)}, u32[]{:S(2)}) collective-permute-start(f32[1,256,384]{2,1,0:T(8,128)S(1)} %get-tuple-element.319), channel_id=1, source_target_pairs={{1,0},{2,1},{3,2},{4,3},{5,4},{6,5},{7,6},{9,8},{10,9},{11,10},{12... | collective-permute-start | bytes 1179656 | tf_op jit(solution)/shard_map/ppermute | solution.py:23
  225.9 51.4 %collective-permute-start.9 = (f32[1,256,384]{2,1,0:T(8,128)S(1)}, f32[1,256,384]{2,1,0:T(8,128)}, u32[]{:S(2)}, u32[]{:S(2)}) collective-permute-start(f32[1,256,384]{2,1,0:T(8,128)S(1)} %get-tuple-element.318), channel_id=1, source_target_pairs={{0,1},{1,2},{2,3},{3,4},{4,5},{5,6},{6,7},{8,9},{9,10},{10,11},{11... | collective-permute-start | bytes 1179656 | tf_op jit(solution)/shard_map/ppermute | solution.py:22
  276.5 117.5 %copy-start.25 = (f32[512,96]{1,0:T(8,128)}, f32[512,96]{1,0:T(8,128)S(1)}, u32[]{:S(2)}) copy-start(f32[512,96]{1,0:T(8,128)S(1)} %all-gather) | copy-start | bytes 589828
  312.1 19.3 %copy-start.1 = (s32[4,256,384]{2,1,0:T(8,128)S(1)}, s32[4,256,384]{2,1,0:T(8,128)}, u32[]{:S(2)}) copy-start(s32[4,256,384]{2,1,0:T(8,128)} %param.6) | copy-start | bytes 4718596
  312.2 19.3 %copy-start.14 = (f32[4,256,384]{2,1,0:T(8,128)S(1)}, f32[4,256,384]{2,1,0:T(8,128)}, u32[]{:S(2)}) copy-start(f32[4,256,384]{2,1,0:T(8,128)} %get-tuple-element.308) | copy-start | bytes 4718596
  340.5 1.1 copy-start.20
  340.5 5.7 copy-start.37
  341.7 53.4 %collective-permute-start.11 = (f32[1,256,384]{2,1,0:T(8,128)S(1)}, f32[1,256,384]{2,1,0:T(8,128)S(1)}, u32[]{:S(2)}, u32[]{:S(2)}) collective-permute-start(f32[1,256,384]{2,1,0:T(8,128)S(1)} %get-tuple-element.316), channel_id=1, source_target_pairs={{0,1},{1,2},{2,3},{3,4},{4,5},{5,6},{6,7},{8,9},{9,10},{10,11},{11... | collective-permute-start | bytes 1179656 | tf_op jit(solution)/shard_map/ppermute | solution.py:22
  344.8 51.0 %collective-permute-start.12 = (f32[1,256,384]{2,1,0:T(8,128)S(1)}, f32[1,256,384]{2,1,0:T(8,128)}, u32[]{:S(2)}, u32[]{:S(2)}) collective-permute-start(f32[1,256,384]{2,1,0:T(8,128)S(1)} %get-tuple-element.317), channel_id=1, source_target_pairs={{1,0},{2,1},{3,2},{4,3},{5,4},{6,5},{7,6},{9,8},{10,9},{11,10},{12... | collective-permute-start | bytes 1179656 | tf_op jit(solution)/shard_map/ppermute | solution.py:23
  394.0 1.0 copy-start.2
  394.0 1.0 copy-start.4
  394.0 1.0 copy-start.6
  394.0 1.0 copy-start.8
  394.0 1.1 copy-start.10
  394.0 2.0 copy-start.21
  412.9 19.3 %copy-start.15 = (f32[4,256,384]{2,1,0:T(8,128)S(1)}, f32[4,256,384]{2,1,0:T(8,128)}, u32[]{:S(2)}) copy-start(f32[4,256,384]{2,1,0:T(8,128)} %get-tuple-element.308) | copy-start | bytes 4718596
  450.4 17.6 %copy-start.26 = (f32[512,96]{1,0:T(8,128)S(1)}, f32[512,96]{1,0:T(8,128)}, u32[]{:S(2)}) copy-start(f32[512,96]{1,0:T(8,128)} %copy-done.25) | copy-start | bytes 589828
  456.2 11.8 %copy-start.3 = (f32[8,64,96]{2,1,0:T(8,128)S(1)}, f32[8,64,96]{2,1,0:T(8,128)}, u32[]{:S(2)}) copy-start(f32[8,64,96]{2,1,0:T(8,128)} %copy-done.2) | copy-start | bytes 589828
  456.2 11.8 %copy-start.5 = (f32[8,64,96]{2,1,0:T(8,128)S(1)}, f32[8,64,96]{2,1,0:T(8,128)}, u32[]{:S(2)}) copy-start(f32[8,64,96]{2,1,0:T(8,128)} %copy-done.4) | copy-start | bytes 589828
  456.2 11.8 %copy-start.7 = (f32[8,64,96]{2,1,0:T(8,128)S(1)}, f32[8,64,96]{2,1,0:T(8,128)}, u32[]{:S(2)}) copy-start(f32[8,64,96]{2,1,0:T(8,128)} %copy-done.6) | copy-start | bytes 589828
  456.2 11.8 %copy-start.9 = (f32[8,64,96]{2,1,0:T(8,128)S(1)}, f32[8,64,96]{2,1,0:T(8,128)}, u32[]{:S(2)}) copy-start(f32[8,64,96]{2,1,0:T(8,128)} %copy-done.8) | copy-start | bytes 589828
  456.2 11.8 %copy-start.11 = (f32[8,64,96]{2,1,0:T(8,128)S(1)}, f32[8,64,96]{2,1,0:T(8,128)}, u32[]{:S(2)}) copy-start(f32[8,64,96]{2,1,0:T(8,128)} %copy-done.10) | copy-start | bytes 589828
  456.2 2.8 collective-permute-start.13
  459.1 3.2 collective-permute-start.14
  462.3 5.6 collective-permute-start.15
  469.7 45.1 %collective-permute-start = (f32[8,64,96]{2,1,0:T(8,128)S(1)}, f32[8,64,96]{2,1,0:T(8,128)S(1)}, u32[]{:S(2)}, u32[]{:S(2)}) collective-permute-start(f32[8,64,96]{2,1,0:T(8,128)S(1)} %fusion.303), channel_id=1, source_target_pairs={{0,8},{8,16},{16,24},{1,9},{9,17},{17,25},{2,10},{10,18},{18,26},{... | collective-permute-start | bytes 589832 | tf_op jit(solution)/shard_map/while/body/eval_jaxpr/ppermute | solution.py:31
  515.7 7.7 %collective-permute-start = (f32[8,64,96]{2,1,0:T(8,128)S(1)}, f32[8,64,96]{2,1,0:T(8,128)S(1)}, u32[]{:S(2)}, u32[]{:S(2)}) collective-permute-start(f32[8,64,96]{2,1,0:T(8,128)S(1)} %fusion.303), channel_id=1, source_target_pairs={{0,8},{8,16},{16,24},{1,9},{9,17},{17,25},{2,10},{10,18},{18,26},{... | collective-permute-start | bytes 589832 | tf_op jit(solution)/shard_map/while/body/eval_jaxpr/ppermute | solution.py:31
  524.3 7.7 %collective-permute-start = (f32[8,64,96]{2,1,0:T(8,128)S(1)}, f32[8,64,96]{2,1,0:T(8,128)S(1)}, u32[]{:S(2)}, u32[]{:S(2)}) collective-permute-start(f32[8,64,96]{2,1,0:T(8,128)S(1)} %fusion.303), channel_id=1, source_target_pairs={{0,8},{8,16},{16,24},{1,9},{9,17},{17,25},{2,10},{10,18},{18,26},{... | collective-permute-start | bytes 589832 | tf_op jit(solution)/shard_map/while/body/eval_jaxpr/ppermute | solution.py:31
  532.9 5.6 copy-start.38
  538.5 11.8 %copy-start.24 = (f32[4,256,384]{2,1,0:T(8,128)S(1)}, f32[4,256,384]{2,1,0:T(8,128)}, u32[]{:S(2)}) copy-start(f32[4,256,384]{2,1,0:T(8,128)} %get-tuple-element.305) | copy-start | bytes 4718596
  550.3 22.0 %copy-start.17 = (f32[1,4,256,384]{3,2,1,0:T(8,128)S(1)}, f32[1,4,256,384]{3,2,1,0:T(8,128)}, u32[]{:S(2)}) copy-start(f32[1,4,256,384]{3,2,1,0:T(8,128)} %param.5) | copy-start | bytes 4718596
  550.4 21.9 %collective-permute-start.16 = (f32[4,256,384]{2,1,0:T(8,128)S(1)}, f32[4,256,384]{2,1,0:T(8,128)S(1)}, u32[]{:S(2)}, u32[]{:S(2)}) collective-permute-start(f32[4,256,384]{2,1,0:T(8,128)S(1)} %broadcast_add_fusion), channel_id=1, source_target_pairs={{0,8},{8,16},{16,24},{1,9},{9,17},{17,25},{2,10},{10,18},{18,26},{... | collective-permute-start | bytes 4718600 | tf_op jit(solution)/shard_map/ppermute | solution.py:31
  (10 other events, 8.6 us)
